TPU v7x, 32 devices: a whole 2x2x4 slice. The times are simulated.
32 devices in a mesh: rep: 2 (over x), inst: 4 (over y, core), tp: 4 (over z).
Axes of the slice: x: 2, y: 2, z: 4, core: 2. Of those that a mesh axis runs over, the one named last changes fastest.
Arguments:
- cache_base: bfloat16 [2, 192, 256, 1024], P(None, ('rep', 'inst'), None, 'tp'), parts along dimension 1, may hold values from -6 to 6
- cache_scale: bfloat16 [2, 192, 8, 1024], P(None, ('rep', 'inst'), None, 'tp'), parts along dimension 1, may hold values from 0.29882812 to 2
- outlier_tiles: bfloat16 [2, 192, 32, 1024], P(None, ('rep', 'inst'), None, 'tp'), parts along dimension 1, may hold values from -8 to 8
- outlier_pos: int32 [2, 192], P(None, 'rep'), parts along dimension 1, may hold values from 0 to 7
- lengths: int32 [192], P('rep'), parts along dimension 0, may hold values from 1 to 256, as said below
- new_slot: int32 [192], P('rep'), parts along dimension 0, may hold values from 0 to 95, as said below
- queries: bfloat16 [2, 192, 8192], P(None, ('rep', 'inst'), 'tp'), parts along dimension 1, may hold values from -68 to 68
- new_kv: bfloat16 [2, 2, 192, 1024], P(None, None, ('rep', 'inst'), 'tp'), parts along dimension 2, may hold values from -6 to 6
- out_weight: bfloat16 [8192, 4096], P('tp'), may hold values from -0.0625 to 0.0625
Outputs:
- attn_out: bfloat16 [2, 192, 4096], P(None, ('rep', 'inst')), parts along dimension 1
There are 2 independent parts, one for each index of `rep`. A program takes and returns all parts, laid end to end along the dimension named above; an argument that names none is the same for every part. Nothing has to cross between parts.
Inputs may be any that keep to these rules, and one draw needn't show every extreme that they name: `lengths`: each instance's requests follow a load level of their own; one request has exactly 256 tokens. A permutation of the 96 slots; slot new_slot[r] lies on instance new_slot[r] // 24, request r starts on instance r // 24. A request either keeps its slot or moves to another instance; from one instance to another move either no requests or exactly 2, and some pair moves 2.
All inputs are finite; a program needn't handle non-finite values.
Results may differ from a plain program's by a relative error of at most 0.012.
The roundings to bfloat16 on the way count: a program that leaves them out, or rounds other values in their place, can miss the bound.
Values may be sent and summed in bfloat16 or wider, within the bound.
A program may use at most 128 MiB of HBM per device.

v0:
```python
import math

import jax
import jax.numpy as jnp
from jax import lax
from jax.sharding import PartitionSpec as P

HD = 128
TILE = 32
MOVE = 2


def dequant_full(bases, scales, outliers, tile_pos):
    batch_rows = bases.shape[1]
    capacity = bases.shape[2]
    feature_width = bases.shape[3]
    tile_size = outliers.shape[2]
    tile_count = capacity // tile_size
    blocks = (
        bases.reshape(2, batch_rows, tile_count, tile_size, feature_width).astype(jnp.float32)
        * scales.astype(jnp.float32)[:, :, :, None, :]
    )
    outlier_hit = jnp.arange(tile_count, dtype=jnp.int32)[None, None, :] == tile_pos[:, :, None]
    blocks = blocks + jnp.where(
        outlier_hit[:, :, :, None, None], outliers.astype(jnp.float32)[:, :, None], 0.0
    )
    return blocks.reshape(bases.shape).astype(jnp.bfloat16)


def attend(queries, fresh_keys, fresh_values, keys_deq, values_deq, slot_lengths, first_step):
    steps_here, batch_rows, query_width = queries.shape
    capacity = keys_deq.shape[1]
    cache_width = keys_deq.shape[2]
    kv_heads = cache_width // HD
    group_size = query_width // cache_width
    block_width = TILE * min(4, capacity // TILE)
    block_count = capacity // block_width
    query_heads = queries.reshape(steps_here, batch_rows, kv_heads, group_size, HD)
    score_scale = 1.0 / math.sqrt(HD)
    live_blocks = (jnp.max(slot_lengths) + block_width - 1) // block_width
    key_blocks = keys_deq.reshape(batch_rows, block_count, block_width, kv_heads, HD)
    value_blocks = values_deq.reshape(batch_rows, block_count, block_width, kv_heads, HD)

    def score_block(block_index, scores):
        key_block = lax.dynamic_index_in_dim(key_blocks, block_index, 1, keepdims=False)
        partial_scores = (
            jnp.einsum(
                "sbgrd,btgd->sbgrt", query_heads, key_block, preferred_element_type=jnp.float32
            )
            * score_scale
        )
        places = block_index * block_width + jnp.arange(block_width, dtype=jnp.int32)
        live_mask = places[None, :] < slot_lengths[:, None]
        partial_scores = jnp.where(live_mask[None, :, None, None, :], partial_scores, -1e30)
        return lax.dynamic_update_index_in_dim(scores, partial_scores, block_index, 0)

    empty_scores = jnp.full(
        (block_count, steps_here, batch_rows, kv_heads, group_size, block_width), -1e30, jnp.float32
    )
    scores = lax.fori_loop(0, live_blocks, score_block, empty_scores)
    new_count = fresh_keys.shape[0]
    fresh_key_heads = fresh_keys.reshape(new_count, batch_rows, kv_heads, HD)
    fresh_value_heads = fresh_values.reshape(new_count, batch_rows, kv_heads, HD)
    new_scores = (
        jnp.einsum(
            "sbgrd,ubgd->sbgru", query_heads, fresh_key_heads, preferred_element_type=jnp.float32
        )
        * score_scale
    )
    visible = (
        jnp.arange(new_count, dtype=jnp.int32)[None, :]
        <= first_step + jnp.arange(steps_here, dtype=jnp.int32)[:, None]
    )
    new_scores = jnp.where(visible[:, None, None, None, :], new_scores, -1e30)
    row_max = jnp.maximum(jnp.max(scores, axis=(0, 5)), jnp.max(new_scores, axis=-1))
    exp_cache = jnp.exp(scores - row_max[None, ..., None])
    exp_new = jnp.exp(new_scores - row_max[..., None])
    denominator = jnp.sum(exp_cache, axis=(0, 5)) + jnp.sum(exp_new, axis=-1)
    weight_cache = (exp_cache / denominator[None, ..., None]).astype(jnp.bfloat16)
    weight_new = (exp_new / denominator[..., None]).astype(jnp.bfloat16)
    context = jnp.einsum(
        "sbgru,ubgd->sbgrd", weight_new, fresh_value_heads, preferred_element_type=jnp.float32
    )

    def value_block(block_index, running):
        value_rows = lax.dynamic_index_in_dim(value_blocks, block_index, 1, keepdims=False)
        block_weights = lax.dynamic_index_in_dim(weight_cache, block_index, 0, keepdims=False)
        return running + jnp.einsum(
            "sbgrt,btgd->sbgrd", block_weights, value_rows, preferred_element_type=jnp.float32
        )

    context = lax.fori_loop(0, live_blocks, value_block, context)
    return context.astype(jnp.bfloat16).reshape(steps_here, batch_rows, query_width)


def run_steps(queries, new_kv, bases, scales, outliers, tile_pos, slot_lengths):
    fresh_keys = new_kv[:, 0]
    fresh_values = new_kv[:, 1]
    dequantized = dequant_full(bases, scales, outliers, tile_pos)
    keys_deq = dequantized[0]
    values_deq = dequantized[1]
    first_ctx = attend(
        queries[0:1], fresh_keys[0:1], fresh_values[0:1], keys_deq, values_deq, slot_lengths, 0
    )
    second_ctx = attend(
        queries[1:2], fresh_keys, fresh_values, keys_deq, values_deq, slot_lengths, 1
    )
    return jnp.concatenate([first_ctx, second_ctx], axis=0)


def on_device(
    cache_base,
    cache_scale,
    outlier_tiles,
    outlier_pos,
    lengths,
    new_slot,
    queries,
    new_kv,
    out_weight,
):
    inst_count = lax.axis_size("inst")
    inst_rank = lax.axis_index("inst")
    slot_count = cache_base.shape[1]
    request_total = new_slot.shape[0]
    bucket_total = inst_count * MOVE
    slot_range = jnp.arange(slot_count, dtype=jnp.int32)
    source = (
        jnp.zeros((request_total,), jnp.int32)
        .at[new_slot]
        .set(jnp.arange(request_total, dtype=jnp.int32))
    )
    held = lax.dynamic_slice_in_dim(source, inst_rank * slot_count, slot_count)
    source_home = held // slot_count
    source_local = held % slot_count
    dest_table = new_slot.reshape(inst_count, slot_count) // slot_count
    my_dest = lax.dynamic_slice_in_dim(new_slot, inst_rank * slot_count, slot_count) // slot_count
    before = slot_range[None, :] < slot_range[:, None]
    out_rank = jnp.sum(before & (my_dest[None, :] == my_dest[:, None]), axis=1)
    leaving = my_dest != inst_rank
    home_rows = dest_table[source_home]
    in_rank = jnp.sum(
        (slot_range[None, :] < source_local[:, None]) & (home_rows == inst_rank), axis=1
    )
    arriving = source_home != inst_rank
    bucket_dest = jnp.arange(bucket_total, dtype=jnp.int32) // MOVE
    bucket_rank = jnp.arange(bucket_total, dtype=jnp.int32) % MOVE
    pick_out = (
        leaving[None, :]
        & (my_dest[None, :] == bucket_dest[:, None])
        & (out_rank[None, :] == bucket_rank[:, None])
    )
    out_slot = jnp.sum(jnp.where(pick_out, slot_range[None, :], 0), axis=1)
    held_pos = jnp.take(outlier_pos, held, axis=1)
    held_lengths = jnp.take(lengths, held)
    arrival_index = source_home * MOVE + in_rank
    send_base = jnp.take(cache_base, out_slot, axis=1)
    send_scale = jnp.take(cache_scale, out_slot, axis=1)
    send_outlier = jnp.take(outlier_tiles, out_slot, axis=1)
    got_base, got_scale, got_outlier = (
        lax.all_to_all(send_base, "inst", split_axis=1, concat_axis=1, tiled=True),
        lax.all_to_all(send_scale, "inst", split_axis=1, concat_axis=1, tiled=True),
        lax.all_to_all(send_outlier, "inst", split_axis=1, concat_axis=1, tiled=True),
    )
    resident_index = jnp.where(arriving, slot_count + arrival_index, source_local)
    resident_base = jnp.take(
        jnp.concatenate([cache_base, got_base], axis=1), resident_index, axis=1
    )
    resident_scale = jnp.take(
        jnp.concatenate([cache_scale, got_scale], axis=1), resident_index, axis=1
    )
    resident_outlier = jnp.take(
        jnp.concatenate([outlier_tiles, got_outlier], axis=1), resident_index, axis=1
    )
    contexts = run_steps(
        queries, new_kv, resident_base, resident_scale, resident_outlier, held_pos, held_lengths
    )
    partial_out = jnp.dot(
        contexts.reshape(-1, contexts.shape[2]), out_weight, preferred_element_type=jnp.float32
    ).reshape(contexts.shape[0], slot_count, -1)
    summed = jnp.stack(
        [lax.psum(partial_out[step_index], "tp") for step_index in range(partial_out.shape[0])]
    )
    return summed.astype(jnp.bfloat16)


def solution(mesh):
    placed = (
        P(None, ("rep", "inst"), None, "tp"),
        P(None, ("rep", "inst"), None, "tp"),
        P(None, ("rep", "inst"), None, "tp"),
        P(None, "rep"),
        P("rep"),
        P("rep"),
        P(None, ("rep", "inst"), "tp"),
        P(None, None, ("rep", "inst"), "tp"),
        P("tp", None),
    )
    return jax.shard_map(
        on_device,
        mesh=mesh,
        in_specs=placed,
        out_specs=P(None, ("rep", "inst"), None),
        check_vma=False,
    )
```

profile of v0, /device:TPU:0, one launch (start us, length us, event | category | flops | bytes accessed | tf_op | source)
XLA Modules:
  0.0 169.1 jit_solution(9486207838933008278)
XLA Ops:
  0.0 0.7 broadcast_divide_fusion
  0.7 0.9 scatter_custom_fusion
  1.6 0.7 compare_and_fusion.3
  2.7 1.5 gather_fusion.4
  4.2 0.7 select_bitcast_fusion.2
  4.9 4.2 %all-to-all-start.1 = ((bf16[2,8,8,256]{3,2,0,1:T(8,128)(2,1)}), bf16[2,8,8,256]{3,2,0,1:T(8,128)(2,1)S(1)}, u32[]{:S(2)}, u32[]{:S(2)}) async-start(bf16[2,8,8,256]{3,2,0,1:T(8,128)(2,1)} %select_bitcast_fusion.2), calls=%async_computation.1 | async-start | bytes 131072 | tf_op jit(solution)/shard_map/all_to_all | solution.py:162
  9.2 0.7 compare_and_fusion.2
  9.9 0.7 fusion.86
  10.6 1.4 fusion.87
  12.0 3.5 %gather_fusion.2 = bf16[8,2,256,256]{3,2,1,0:T(8,128)(2,1)S(1)} fusion(bf16[2,24,256,256]{3,2,1,0:T(8,128)(2,1)} %param.17, s32[1024]{0:T(1024)S(1)} %pad_clamp_fusion.1), kind=kCustom, calls=%fused_computation.2 | custom fusion | bytes 4194336 | tf_op jit(solution)/shard_map/jit(_take)/gather | solution.py:157
  15.5 1.6 select_bitcast_fusion
  17.3 0.6 gather_fusion.7
  17.9 0.8 select_bitcast_fusion.1
  18.8 0.6 gather_fusion.6
  19.6 0.6 gather_fusion.1
  20.4 0.7 gather_fusion
  21.1 3.4 %all-to-all-start.2 = ((bf16[2,8,32,256]{3,2,0,1:T(8,128)(2,1)}), bf16[2,8,32,256]{3,2,0,1:T(8,128)(2,1)S(1)}, u32[]{:S(2)}, u32[]{:S(2)}) async-start(bf16[2,8,32,256]{3,2,0,1:T(8,128)(2,1)} %select_bitcast_fusion.1), calls=%async_computation.2 | async-start | bytes 524288 | tf_op jit(solution)/shard_map/all_to_all | solution.py:163
  24.5 0.6 fusion.83
  26.1 0.6 reshape.438
  26.7 0.6 reshape.347
  27.4 0.6 reshape_squeeze.17
  28.1 2.5 %all-to-all-done.2 = bf16[2,8,32,256]{3,2,0,1:T(8,128)(2,1)S(1)} async-done(((bf16[2,8,32,256]{3,2,0,1:T(8,128)(2,1)}), bf16[2,8,32,256]{3,2,0,1:T(8,128)(2,1)S(1)}, u32[]{:S(2)}, u32[]{:S(2)}) %all-to-all-start.2) | async-done | bytes 262176 | tf_op jit(solution)/shard_map/all_to_all | solution.py:163
  30.5 3.6 %all-to-all-start = ((bf16[2,8,256,256]{3,2,0,1:T(8,128)(2,1)}), bf16[2,8,256,256]{3,2,0,1:T(8,128)(2,1)S(1)}, u32[]{:S(2)}, u32[]{:S(2)}) async-start(bf16[2,8,256,256]{3,2,0,1:T(8,128)(2,1)} %select_bitcast_fusion), calls=%async_computation | async-start | bytes 4194304 | tf_op jit(solution)/shard_map/all_to_all | solution.py:161
  34.2 0.8 fusion.89
  35.0 1.4 fusion.88
  36.4 1.6 pad_maximum_fusion.3
  38.1 2.2 %gather_fusion.5 = bf16[24,2,8,256]{3,2,1,0:T(8,128)(2,1)} fusion(bf16[2,32,8,256]{3,2,1,0:T(8,128)(2,1)} %pad_maximum_fusion.3, s32[1024]{0:T(1024)S(1)} %pad_clamp_fusion), kind=kCustom, calls=%fused_computation.5 | custom fusion | bytes 393312 | tf_op jit(solution)/shard_map/jit(_take)/gather | solution.py:169
  40.3 1.8 %convert_bitcast_fusion.1 = f32[2,24,8,256]{3,2,0,1:T(8,128)} fusion(bf16[24,2,8,256]{3,2,1,0:T(8,128)(2,1)} %gather_fusion.5, pred[24]{0:T(512)(128)(4,1)S(1)} %get-tuple-element.223), kind=kLoop, calls=%fused_computation.64 | loop fusion | flops 196608 | bytes 589848 | tf_op jit(solution)/shard_map/convert_element_type | solution.py:21
  42.0 1.1 pad_maximum_fusion.1
  43.1 1.8 %gather_fusion.8 = bf16[24,2,32,256]{3,2,1,0:T(8,128)(2,1)S(1)} fusion(bf16[2,32,32,256]{3,2,1,0:T(8,128)(2,1)} %pad_maximum_fusion.1, s32[1024]{0:T(1024)S(1)} %pad_clamp_fusion), kind=kCustom, calls=%fused_computation.8 | custom fusion | bytes 1572960 | tf_op jit(solution)/shard_map/jit(_take)/gather | solution.py:172
  44.9 1.3 convert_bitcast_fusion
  46.3 13.5 %all-to-all-done = bf16[2,8,256,256]{3,2,0,1:T(8,128)(2,1)S(1)} async-done(((bf16[2,8,256,256]{3,2,0,1:T(8,128)(2,1)}), bf16[2,8,256,256]{3,2,0,1:T(8,128)(2,1)S(1)}, u32[]{:S(2)}, u32[]{:S(2)}) %all-to-all-start) | async-done | bytes 2097184 | tf_op jit(solution)/shard_map/all_to_all | solution.py:161
  59.8 6.7 %pad_maximum_fusion = bf16[2,32,256,256]{3,2,1,0:T(8,128)(2,1)} fusion(bf16[2,24,256,256]{3,2,1,0:T(8,128)(2,1)} %param.17, bf16[2,8,256,256]{3,2,0,1:T(8,128)(2,1)S(1)} %all-to-all-done), kind=kLoop, calls=%fused_computation.54 | loop fusion | flops 16777216 | bytes 16777216 | tf_op jit(solution)/shard_map/concatenate | solution.py:167
  66.6 8.0 %gather_fusion.3 = bf16[24,2,256,256]{3,2,1,0:T(8,128)(2,1)} fusion(bf16[2,32,256,256]{3,2,1,0:T(8,128)(2,1)} %pad_maximum_fusion, s32[1024]{0:T(1024)S(1)} %pad_clamp_fusion), kind=kCustom, calls=%fused_computation.3 | custom fusion | bytes 12583008 | tf_op jit(solution)/shard_map/jit(_take)/gather | solution.py:166
  74.6 6.7 %fusion.65 = bf16[2,24,256,256]{3,2,0,1:T(8,128)(2,1)S(1)} fusion(bf16[24,2,256,256]{3,2,1,0:T(8,128)(2,1)} %gather_fusion.3, f32[2,24,32,256]{3,2,0,1:T(8,128)S(1)} %copy-done.2, f32[2,24,8,256]{3,2,0,1:T(8,128)S(1)} %copy-done.6, pred[24]{0:T(512)(128)(4,1)S(1)} %get-tuple-element.223, pred[2,24,256]{2,0,1:T(4,128)(4,1)S(1)} %copy.27), kind=kLoop, calls=%fused_computation.52 | loop fusion | flops 18874368 | bytes 14561304 | tf_op jit(solution)/shard_map/convert_element_type | solution.py:27
  81.3 2.2 %fusion.84 = (bf16[1,24,256,256]{3,2,0,1:T(8,128)(2,1)}, bf16[1,24,256,256]{3,2,0,1:T(8,128)(2,1)S(1)}) fusion(bf16[2,24,256,256]{3,2,0,1:T(8,128)(2,1)S(1)} %fusion.65), kind=kLoop, calls=%fused_computation.134 | loop fusion | bytes 12582912 | tf_op jit(solution)/shard_map/slice | solution.py:101
  83.6 3.0 %reshape_squeeze.14 = bf16[24,2,128,2,128]{4,3,2,1,0:T(2,128)(2,1)} reshape(bf16[1,24,256,256]{3,2,0,1:T(8,128)(2,1)S(1)} %get-tuple-element.232) | data formatting | bytes 6291456 | tf_op jit(solution)/shard_map/reshape;squeeze | solution.py:41
  86.6 2.7 %copy.29 = bf16[24,2,128,2,128]{4,2,3,0,1:T(8,128)(2,1)S(1)} copy(bf16[24,2,128,2,128]{4,3,2,1,0:T(2,128)(2,1)} %reshape_squeeze.14) | data formatting | bytes 6291456 | tf_op jit(solution)/shard_map/while | solution.py:60
  89.3 3.8 %while.40 = (s32[]{:T(128)}, f32[2,1,24,2,8,128]{5,4,3,2,1,0:T(8,128)S(1)}, s32[]{:T(128)}, s32[24]{0:T(128)S(1)}, bf16[24,2,128,2,128]{4,2,3,0,1:T(8,128)(2,1)S...) while((s32[]{:T(128)}, ...), condition=%wide.region_6.7_spmd, body=%wide.region_5.6_spmd.sunk | while | flops 12684422 | bytes 1876215 | solution.py:60
  89.4 1.8 %fusion.113 = f32[2,1,24,2,8,128]{5,4,3,2,1,0:T(8,128)S(1)} fusion(f32[2,1,24,2,8,128]{5,4,3,2,1,0:T(8,128)S(1)} %get-tuple-element.457, s32[]{:T(128)S(6)} %select_n.280, bf16[24,2,128,2,128]{4,2,3,0,1:T(8,128)(2,1)S(1)} %get-tuple-element.470, bf16[1,24,2,8,128]{4,3,2,1,0:T(8,128)(2,1)} %get-tuple-element.471, ...), kind=kOutput, calls=%fused_computation.17.clone.1 | convolution fusion | flops 12681216 | bytes 1871872 | tf_op jit(solution)/shard_map/while/body/sbgrd,btgd->sbgrt/dot_general | solution.py:47
  91.3 1.8 %fusion.113 = f32[2,1,24,2,8,128]{5,4,3,2,1,0:T(8,128)S(1)} fusion(f32[2,1,24,2,8,128]{5,4,3,2,1,0:T(8,128)S(1)} %get-tuple-element.457, s32[]{:T(128)S(6)} %select_n.280, bf16[24,2,128,2,128]{4,2,3,0,1:T(8,128)(2,1)S(1)} %get-tuple-element.470, bf16[1,24,2,8,128]{4,3,2,1,0:T(8,128)(2,1)} %get-tuple-element.471, ...), kind=kOutput, calls=%fused_computation.17.clone.1 | convolution fusion | flops 12681216 | bytes 1871872 | tf_op jit(solution)/shard_map/while/body/sbgrd,btgd->sbgrt/dot_general | solution.py:47
  93.1 0.8 reduce_max.36
  93.9 0.8 multiply_maximum_fusion
  94.7 0.2 fusion.69
  94.9 1.4 fusion.82
  96.3 0.9 divide_convert_fusion.1
  97.2 5.5 %reshape_squeeze.15 = bf16[24,2,128,2,128]{4,3,2,1,0:T(2,128)(2,1)} reshape(bf16[1,24,256,256]{3,2,0,1:T(8,128)(2,1)} %get-tuple-element.231) | data formatting | bytes 6291456 | tf_op jit(solution)/shard_map/reshape;squeeze | solution.py:42
  102.7 4.4 %copy.30 = bf16[24,2,128,2,128]{4,2,3,0,1:T(8,128)(2,1)} copy(bf16[24,2,128,2,128]{4,3,2,1,0:T(2,128)(2,1)} %reshape_squeeze.15) | data formatting | bytes 6291456 | tf_op jit(solution)/shard_map/while | solution.py:92
  107.2 3.9 %while.41 = (s32[]{:T(128)}, f32[1,24,2,8,128]{4,3,2,1,0:T(8,128)S(1)}, s32[]{:T(128)}, bf16[24,2,128,2,128]{4,2,3,0,1:T(8,128)(2,1)}, bf16[2,1,24,2,8,128]{5,4,...) while((s32[]{:T(128)}, f32[1,24,2,8,128]{4,3,2,1,0:T(8,128)S(1)}, s32[]{:T(128)}, ...), condition=%wide.region_10.11_spmd, body=%wide.region_9.10_spmd.sunk | while | flops 12632069 | bytes 2065527 | solution.py:92
  107.3 1.9 %fusion.116 = f32[1,24,2,8,128]{4,3,2,1,0:T(8,128)S(1)} fusion(f32[1,24,2,8,128]{4,3,2,1,0:T(8,128)S(1)} %get-tuple-element.485, bf16[24,2,128,2,128]{4,2,3,0,1:T(8,128)(2,1)} %get-tuple-element.495, s32[]{:T(128)S(6)} %select_n.281, bf16[2,1,24,2,8,128]{5,4,3,2,1,0:T(8,128)(2,1)S(1)} %get-tuple-element.496), kind=kOutput, calls=%fused_computation.26.clone.1 | convolution fusion | flops 12632064 | bytes 2065408 | tf_op jit(solution)/shard_map/while/body/sbgrt,btgd->sbgrd/dot_general | solution.py:88
  109.2 1.9 %fusion.116 = f32[1,24,2,8,128]{4,3,2,1,0:T(8,128)S(1)} fusion(f32[1,24,2,8,128]{4,3,2,1,0:T(8,128)S(1)} %get-tuple-element.485, bf16[24,2,128,2,128]{4,2,3,0,1:T(8,128)(2,1)} %get-tuple-element.495, s32[]{:T(128)S(6)} %select_n.281, bf16[2,1,24,2,8,128]{5,4,3,2,1,0:T(8,128)(2,1)S(1)} %get-tuple-element.496), kind=kOutput, calls=%fused_computation.26.clone.1 | convolution fusion | flops 12632064 | bytes 2065408 | tf_op jit(solution)/shard_map/while/body/sbgrt,btgd->sbgrd/dot_general | solution.py:88
  111.1 0.7 reshape.341
  111.9 3.8 %while.42 = (s32[]{:T(128)}, f32[2,1,24,2,8,128]{5,4,3,2,1,0:T(8,128)S(1)}, s32[]{:T(128)}, s32[24]{0:T(128)S(1)}, bf16[24,2,128,2,128]{4,2,3,0,1:T(8,128)(2,1)S...) while((s32[]{:T(128)}, ...), condition=%wide.region_12.13_spmd, body=%wide.region_11.12_spmd.sunk | while | flops 12684422 | bytes 1876215 | solution.py:60
  112.0 1.8 %fusion.119 = f32[2,1,24,2,8,128]{5,4,3,2,1,0:T(8,128)S(1)} fusion(f32[2,1,24,2,8,128]{5,4,3,2,1,0:T(8,128)S(1)} %get-tuple-element.403, s32[]{:T(128)S(6)} %select_n.283, bf16[24,2,128,2,128]{4,2,3,0,1:T(8,128)(2,1)S(1)} %get-tuple-element.416, bf16[1,24,2,8,128]{4,3,2,1,0:T(8,128)(2,1)} %get-tuple-element.417, ...), kind=kOutput, calls=%fused_computation.37.clone.1 | convolution fusion | flops 12681216 | bytes 1871872 | tf_op jit(solution)/shard_map/while/body/sbgrd,btgd->sbgrt/dot_general | solution.py:47
  113.9 1.8 %fusion.119 = f32[2,1,24,2,8,128]{5,4,3,2,1,0:T(8,128)S(1)} fusion(f32[2,1,24,2,8,128]{5,4,3,2,1,0:T(8,128)S(1)} %get-tuple-element.403, s32[]{:T(128)S(6)} %select_n.283, bf16[24,2,128,2,128]{4,2,3,0,1:T(8,128)(2,1)S(1)} %get-tuple-element.416, bf16[1,24,2,8,128]{4,3,2,1,0:T(8,128)(2,1)} %get-tuple-element.417, ...), kind=kOutput, calls=%fused_computation.37.clone.1 | convolution fusion | flops 12681216 | bytes 1871872 | tf_op jit(solution)/shard_map/while/body/sbgrd,btgd->sbgrt/dot_general | solution.py:47
  115.8 0.8 max.22
  116.9 0.9 fusion.71
  118.0 1.0 convolution_bitcast_fusion
  119.0 3.9 %while.43 = (s32[]{:T(128)}, f32[1,24,2,8,128]{4,3,2,1,0:T(8,128)S(1)}, s32[]{:T(128)}, bf16[24,2,128,2,128]{4,2,3,0,1:T(8,128)(2,1)}, bf16[2,1,24,2,8,128]{5,4,...) while((s32[]{:T(128)}, f32[1,24,2,8,128]{4,3,2,1,0:T(8,128)S(1)}, s32[]{:T(128)}, ...), condition=%wide.region_18.19_spmd, body=%wide.region_17.18_spmd.sunk | while | flops 12632069 | bytes 2065527 | solution.py:92
  119.1 2.0 %fusion.122 = f32[1,24,2,8,128]{4,3,2,1,0:T(8,128)S(1)} fusion(f32[1,24,2,8,128]{4,3,2,1,0:T(8,128)S(1)} %get-tuple-element.431, bf16[24,2,128,2,128]{4,2,3,0,1:T(8,128)(2,1)} %get-tuple-element.441, s32[]{:T(128)S(6)} %select_n.284, bf16[2,1,24,2,8,128]{5,4,3,2,1,0:T(8,128)(2,1)S(1)} %get-tuple-element.442), kind=kOutput, calls=%fused_computation.46.clone.1 | convolution fusion | flops 12632064 | bytes 2065408 | tf_op jit(solution)/shard_map/while/body/sbgrt,btgd->sbgrd/dot_general | solution.py:88
  121.0 1.9 %fusion.122 = f32[1,24,2,8,128]{4,3,2,1,0:T(8,128)S(1)} fusion(f32[1,24,2,8,128]{4,3,2,1,0:T(8,128)S(1)} %get-tuple-element.431, bf16[24,2,128,2,128]{4,2,3,0,1:T(8,128)(2,1)} %get-tuple-element.441, s32[]{:T(128)S(6)} %select_n.284, bf16[2,1,24,2,8,128]{5,4,3,2,1,0:T(8,128)(2,1)S(1)} %get-tuple-element.442), kind=kOutput, calls=%fused_computation.46.clone.1 | convolution fusion | flops 12632064 | bytes 2065408 | tf_op jit(solution)/shard_map/while/body/sbgrt,btgd->sbgrd/dot_general | solution.py:88
  123.1 8.8 %fusion.90 = f32[48,4096]{1,0:T(8,128)S(1)} fusion(bf16[48,2048]{1,0:T(8,128)(2,1)S(1)} %bitcast.229, bf16[2048,4096]{1,0:T(8,128)(2,1)} %param.25), kind=kOutput, calls=%fused_computation.140 | convolution fusion | flops 805306368 | bytes 17760256 | tf_op jit(solution)/shard_map/dot_general | solution.py:178
  131.9 36.3 %all-reduce.2 = (bf16[24,4096]{1,0:T(8,128)(2,1)S(1)}, bf16[24,4096]{1,0:T(8,128)(2,1)S(1)}) all-reduce(f32[24,4096]{1,0:T(8,128)S(1)} %get-tuple-element.234, f32[24,4096]{1,0:T(8,128)S(1)} %get-tuple-element.233), channel_id=1, replica_groups=mesh['rep'=2,'inst'=4,'tp'=4] {'tp'}, use_global_device_ids=true, to_apply=%region_20.21 | all-reduce | flops 196608 | bytes 1179648 | tf_op jit(solution)/shard_map/psum | solution.py:182
  168.3 0.8 pad_maximum_fusion.2
  (81 shorter events, 2.9 us)
Async XLA Ops:
  0.0 20.4 %copy-start = (s32[96]{0:T(128)S(1)}, s32[96]{0:T(128)}, u32[]{:S(2)}) copy-start(s32[96]{0:T(128)} %param.21) | copy-start | bytes 1156
  4.9 16.2 %all-to-all-start.1 = ((bf16[2,8,8,256]{3,2,0,1:T(8,128)(2,1)}), bf16[2,8,8,256]{3,2,0,1:T(8,128)(2,1)S(1)}, u32[]{:S(2)}, u32[]{:S(2)}) async-start(bf16[2,8,8,256]{3,2,0,1:T(8,128)(2,1)} %select_bitcast_fusion.2), calls=%async_computation.1 | async-start | bytes 131072 | tf_op jit(solution)/shard_map/all_to_all | solution.py:162
  15.5 1.8 %copy-start.7 = (bf16[2,24,32,256]{3,2,1,0:T(8,128)(2,1)S(1)}, bf16[2,24,32,256]{3,2,1,0:T(8,128)(2,1)}, u32[]{:S(2)}) copy-start(bf16[2,24,32,256]{3,2,1,0:T(8,128)(2,1)} %param.19) | copy-start | bytes 2359300
  15.5 3.2 %copy-start.15 = (s32[2,96]{1,0:T(2,128)S(1)}, s32[2,96]{1,0:T(2,128)}, u32[]{:S(2)}) copy-start(s32[2,96]{1,0:T(2,128)} %param.20) | copy-start | bytes 2308
  15.5 4.1 %copy-start.9 = (bf16[2,24,2048]{2,1,0:T(8,128)(2,1)S(1)}, bf16[2,24,2048]{2,1,0:T(8,128)(2,1)}, u32[]{:S(2)}) copy-start(bf16[2,24,2048]{2,1,0:T(8,128)(2,1)} %param.23) | copy-start | bytes 589828
  17.1 10.3 %copy-start.11 = (bf16[2,1,24,256]{3,2,1,0:T(8,128)(2,1)S(1)}, bf16[2,1,24,256]{3,2,1,0:T(8,128)(2,1)}, u32[]{:S(2)}) copy-start(bf16[2,1,24,256]{3,2,1,0:T(8,128)(2,1)} %get-tuple-element.241) | copy-start | bytes 73732
  17.1 10.3 %copy-start.10 = (bf16[2,1,24,256]{3,2,1,0:T(8,128)(2,1)S(1)}, bf16[2,1,24,256]{3,2,1,0:T(8,128)(2,1)}, u32[]{:S(2)}) copy-start(bf16[2,1,24,256]{3,2,1,0:T(8,128)(2,1)} %get-tuple-element.242) | copy-start | bytes 73732
  21.1 9.4 %all-to-all-start.2 = ((bf16[2,8,32,256]{3,2,0,1:T(8,128)(2,1)}), bf16[2,8,32,256]{3,2,0,1:T(8,128)(2,1)S(1)}, u32[]{:S(2)}, u32[]{:S(2)}) async-start(bf16[2,8,32,256]{3,2,0,1:T(8,128)(2,1)} %select_bitcast_fusion.1), calls=%async_computation.2 | async-start | bytes 524288 | tf_op jit(solution)/shard_map/all_to_all | solution.py:163
  26.1 16.0 %copy-start.4 = (bf16[3,8,16,128]{3,2,1,0:T(8,128)(2,1)}, bf16[3,8,16,128]{3,2,1,0:T(8,128)(2,1)S(1)}, u32[]{:S(2)}) copy-start(bf16[3,8,16,128]{3,2,1,0:T(8,128)(2,1)S(1)} %copy.37) | copy-start | bytes 294916
  27.4 14.7 %copy-start.3 = (bf16[3,8,16,128]{3,2,1,0:T(8,128)(2,1)}, bf16[3,8,16,128]{3,2,1,0:T(8,128)(2,1)S(1)}, u32[]{:S(2)}) copy-start(bf16[3,8,16,128]{3,2,1,0:T(8,128)(2,1)S(1)} %copy.39) | copy-start | bytes 294916
  27.4 6.8 %copy-start.14 = (bf16[24,2,128,1]{2,3,1,0:T(2,128)(2,1)S(1)}, bf16[24,2,128,1]{2,3,1,0:T(2,128)(2,1)}, u32[]{:S(2)}) copy-start(bf16[24,2,128,1]{2,3,1,0:T(2,128)(2,1)} %reshape.438) | copy-start | bytes 36868
  30.5 29.3 %all-to-all-start = ((bf16[2,8,256,256]{3,2,0,1:T(8,128)(2,1)}), bf16[2,8,256,256]{3,2,0,1:T(8,128)(2,1)S(1)}, u32[]{:S(2)}, u32[]{:S(2)}) async-start(bf16[2,8,256,256]{3,2,0,1:T(8,128)(2,1)} %select_bitcast_fusion), calls=%async_computation | async-start | bytes 4194304 | tf_op jit(solution)/shard_map/all_to_all | solution.py:161
  66.6 8.0 %copy-start.2 = (f32[2,24,32,256]{3,2,0,1:T(8,128)S(1)}, f32[2,24,32,256]{3,2,0,1:T(8,128)}, u32[]{:S(2)}) copy-start(f32[2,24,32,256]{3,2,0,1:T(8,128)} %convert_bitcast_fusion) | copy-start | bytes 4718596
  66.6 8.0 %copy-start.6 = (f32[2,24,8,256]{3,2,0,1:T(8,128)S(1)}, f32[2,24,8,256]{3,2,0,1:T(8,128)}, u32[]{:S(2)}) copy-start(f32[2,24,8,256]{3,2,0,1:T(8,128)} %convert_bitcast_fusion.1) | copy-start | bytes 1179652
  102.7 4.4 %copy-start.12 = (f32[24,2,128]{2,1,0:T(2,128)S(1)}, f32[24,2,128]{2,1,0:T(2,128)}, u32[]{:S(2)}) copy-start(f32[24,2,128]{2,1,0:T(2,128)} %reshape.347) | copy-start | bytes 73732
  102.7 4.4 %copy-start.13 = (f32[24,2,8]{2,1,0:T(2,128)S(1)}, f32[24,2,8]{2,1,0:T(2,128)}, u32[]{:S(2)}) copy-start(f32[24,2,8]{2,1,0:T(2,128)} %get-tuple-element.238) | copy-start | bytes 4612
  102.7 4.6 %copy-start.5 = (bf16[2,1,24,2,8,128]{5,4,3,2,1,0:T(8,128)(2,1)S(1)}, bf16[2,1,24,2,8,128]{5,4,3,2,1,0:T(8,128)(2,1)}, u32[]{:S(2)}) copy-start(bf16[2,1,24,2,8,128]{5,4,3,2,1,0:T(8,128)(2,1)} %divide_convert_fusion.1) | copy-start | bytes 589828
  119.0 4.0 %copy-start.8 = (bf16[1,24,2048]{2,1,0:T(8,128)(2,1)S(1)}, bf16[1,24,2048]{2,1,0:T(8,128)(2,1)}, u32[]{:S(2)}) copy-start(bf16[1,24,2048]{2,1,0:T(8,128)(2,1)} %reshape.341) | copy-start | bytes 294916
  123.1 46.0 %copy-start.1 = (s32[96]{0:T(128)S(1)}, s32[96]{0:T(128)}, u32[]{:S(2)}) copy-start(s32[96]{0:T(128)} %param.21) | copy-start | bytes 1156
where the time goes:
time: 171 us; the launch traced here: 169 us
  local copies, waits for them, and re-layouts  43 us (25%)
  blocking collectives  36.3 us (21%)
  other arithmetic  34.3 us (20%)
  matrix products  27 us (16%)
  waiting for transfers between devices  16 us (9%)
  starting transfers between devices  11.3 us (7%)
    psum x1, blocking collectives, on_device(): lax.psum(partial_out[step_index], 'tp')  36.3 us
    all_to_all x1, waiting for transfers between devices, on_device(): lax.all_to_all(send_base, 'inst', split_axis=1, concat_axis=1, tiled=True)  13.5 us
    dot_general x1, matrix products, on_device(): jnp.dot(contexts.reshape(-1, contexts.shape[2]), out_weight, preferred_el...  8.79 us
    gather x1, local copies, waits for them, and re-layouts, on_device(): jnp.take(jnp.concatenate([cache_base, got_base], axis=1), resident_index,...  8.02 us
    dot_general x4, matrix products, value_block(): jnp.einsum('sbgrt,btgd->sbgrd', block_weights, value_rows, preferred_elem...  7.73 us
    dot_general x4, matrix products, score_block(): jnp.einsum('sbgrd,btgd->sbgrt', query_heads, key_block, preferred_element...  7.23 us
    concatenate x1, other arithmetic, on_device(): jnp.concatenate([cache_base, got_base], axis=1)  6.75 us
    convert_element_type x1, other arithmetic, dequant_full(): return blocks.reshape(bases.shape).astype(jnp.bfloat16)  6.74 us
  transfers between devices with their start and end apart: 3, of which 2 were waited for; matrix products, arithmetic and copies ran while one was open for 16% of the time, Pallas kernels for 0%

commit v1 on v0

v1 whole, which is shorter than its diff:
```python
import functools
import math

import jax
import jax.numpy as jnp
from jax import lax
from jax.experimental import pallas as pl
from jax.experimental.pallas import tpu as pltpu
from jax.sharding import PartitionSpec as P

HD = 128
TILE = 32
MOVE = 2
PARTS = 4
MESH = pl.DeviceIdType.MESH
F32 = jnp.float32
BF16 = jnp.bfloat16


def iota(shape, dim):
    return lax.broadcasted_iota(jnp.int32, shape, dim)


def split(values, size, count):
    quotient = jnp.zeros_like(values)
    for i in range(1, count):
        quotient = quotient + jnp.where(values >= i * size, 1, 0)
    return quotient


def onehot(mask):
    return jnp.where(mask, 1.0, 0.0).astype(BF16)


def nt(a, b):
    return lax.dot_general(a, b, (((1,), (1,)), ((), ())), preferred_element_type=F32)


def nn(a, b):
    return jnp.dot(a, b, preferred_element_type=F32)


def body(
    dims,
    ns_ref, pos_ref, len_ref, q_ref, kv_ref, base_hbm, scale_hbm, outl_hbm, w_hbm,
    out_ref,
    cache, scale, outl, wbuf, qsend, qrecv, q3, kn, c3, lhs,
    msend, mrecv, own, bsend, brecv,
    load_sem, w_sem, qs_sem, qr_sem, ms_sem, mr_sem, bs_sem, br_sem, as_sem, ar_sem,
):
    n_inst, n_tp, slots, steps, chunk, per = dims
    me_i = lax.axis_index("inst")
    me_t = lax.axis_index("tp")
    n_req = ns_ref.shape[1]
    q_width = q_ref.shape[1]
    width = kv_ref.shape[1]
    cap = cache.shape[2]
    tiles = cap // TILE
    heads = width // HD
    group = q_width // width
    rows = q_width // HD * steps
    piece = q_width // PARTS
    block = wbuf.shape[2]
    quarter = block // PARTS
    bucket = steps * MOVE * PARTS
    n_bucket = n_inst * bucket
    flat = steps * slots
    chunks = slots // chunk
    first = me_i * slots

    n_dev = n_inst * n_tp
    me = me_i * n_tp + me_t
    barrier = pltpu.get_barrier_semaphore()

    @pl.loop(1, n_dev)
    def _(offset):
        other = lax.rem(me + offset, n_dev)
        pl.semaphore_signal(
            barrier, inc=1,
            device_id={"inst": other // n_tp, "tp": lax.rem(other, n_tp)},
            device_id_type=MESH,
        )

    def load_cache(which, part):
        span = pl.ds(part * chunk, chunk)
        return pltpu.make_async_copy(
            base_hbm.at[which, span], cache.at[which, span], load_sem.at[which * chunks + part]
        )

    load_scale = pltpu.make_async_copy(scale_hbm, scale, load_sem.at[2 * chunks])
    load_outl = pltpu.make_async_copy(outl_hbm, outl, load_sem.at[2 * chunks + 1])

    def load_weight(k):
        col = lax.rem(me_t + 1 + k, n_tp)
        return pltpu.make_async_copy(
            w_hbm.at[:, pl.ds(pl.multiple_of(col * block, block), block)], wbuf.at[k], w_sem.at[k]
        )

    load_scale.start()
    load_outl.start()
    for which in range(2):
        for part in range(chunks):
            load_cache(which, part).start()
    for k in range(n_tp):
        load_weight(k).start()

    ns = ns_ref[...]
    lane = iota((1, n_req), 1)
    home = split(lane, slots, n_inst)
    dest = split(ns, slots, n_inst)
    code = (home * n_inst + dest).astype(F32)
    row_i = iota((n_req, n_req), 0)
    col_i = iota((n_req, n_req), 1)
    code_all = jnp.broadcast_to(code, (n_req, n_req))
    code_col = jnp.sum(jnp.where(row_i == col_i, code_all, 0.0), axis=1, keepdims=True)
    rank = jnp.sum(
        jnp.where(jnp.logical_and(code_col == code_all, row_i < col_i), 1.0, 0.0),
        axis=0, keepdims=True,
    )

    def bucket_fields(shape, dim):
        index = iota(shape, dim)
        return index >> 4, (index >> 3) & 1, (index >> 2) & 1, index & 3

    b_inst, _, b_rank, _ = bucket_fields((n_bucket, n_req), 0)
    same_rank = jnp.logical_and(rank == b_rank.astype(F32), b_inst != me_i)
    arriving = onehot(same_rank & (home == b_inst) & (dest == me_i))
    leaving = onehot(same_rank & (dest == b_inst) & (home == me_i))

    def slot_rows(count):
        index = iota((count * slots, n_req), 0)
        return index - slots * split(index, slots, count)

    slot_steps = onehot(ns - first == slot_rows(steps))
    slot_kv = onehot(ns - first == slot_rows(2 * steps))
    local = onehot(lane - first == slot_rows(steps))

    def step_of(shape, dim):
        return split(iota(shape, dim), slots, steps)

    def fresh_of(shape, dim):
        index = split(iota(shape, dim), slots, 2 * steps)
        return index >> 1, index & 1

    def keep(mask, values):
        return jnp.where(mask, values, 0.0).astype(BF16)

    shape = (n_bucket, flat)
    _, b_step, _, b_part = bucket_fields(shape, 0)
    pick = keep(b_step == step_of(shape, 1), nt(arriving, slot_steps))
    total = jnp.zeros((n_bucket, piece), F32)
    for x in range(PARTS):
        sel = jnp.where(b_part == x, pick.astype(F32), 0.0).astype(BF16)
        total = total + nn(sel, q_ref[:, x * piece:(x + 1) * piece])
    qsend[:, :, :piece] = total.astype(BF16).reshape(n_inst, bucket, piece)
    shape = (n_bucket, 2 * flat)
    _, b_step, _, b_part = bucket_fields(shape, 0)
    f_step, f_kv = fresh_of(shape, 1)
    pick = jnp.where(b_step == f_step, nt(arriving, slot_kv), 0.0)
    total = jnp.zeros((n_bucket, HD), F32)
    for which in range(2):
        for g in range(heads):
            sel = keep((f_kv == which) & (b_part == which * heads + g), pick)
            total = total + nn(sel, kv_ref[:, g * HD:(g + 1) * HD])
    qsend[:, :, piece:] = total.astype(BF16).reshape(n_inst, bucket, HD)
    qrecv[me_i] = jnp.zeros((bucket, piece + HD), BF16)
    brecv[me_i] = jnp.zeros((n_tp, bucket, quarter), BF16)

    pl.semaphore_wait(barrier, n_dev - 1)

    def query_copy(other, slot):
        return pltpu.make_async_remote_copy(
            src_ref=qsend.at[other], dst_ref=qrecv.at[slot],
            send_sem=qs_sem.at[other], recv_sem=qr_sem.at[slot],
            device_id={"inst": other, "tp": me_t}, device_id_type=MESH,
        )

    for offset in range(1, n_inst):
        query_copy(lax.rem(me_i + offset, n_inst), me_i).start()

    load_scale.wait()
    load_outl.wait()

    def dequantize(which, start):
        scales = scale[which, pl.ds(pl.multiple_of(start * tiles, per * tiles), per * tiles), :]
        scales = scales.astype(F32)
        for i in range(per):
            request = start + i
            place = pos_ref[which, first + request]
            extra = outl[which, request].astype(F32)
            for t in range(tiles):
                values = cache[which, request, t * TILE:(t + 1) * TILE, :].astype(F32)
                values = values * scales[i * tiles + t:i * tiles + t + 1, :]
                values = values + jnp.where(place == t, extra, 0.0)
                cache[which, request, t * TILE:(t + 1) * TILE, :] = values.astype(BF16)

    @pl.loop(0, chunks)
    def _(part):
        load_cache(0, part).wait()

        @pl.loop(0, chunk // per)
        def _(p):
            dequantize(0, part * chunk + p * per)

    for offset in range(1, n_inst):
        other = lax.rem(me_i + offset, n_inst)
        copy = query_copy(other, other)
        copy.wait_send()
        copy.wait_recv()
    got = qrecv[...].reshape(n_bucket, piece + HD)
    shape = (flat, n_bucket)
    _, b_step, _, b_part = bucket_fields(shape, 1)
    moved = jnp.where(b_step == step_of(shape, 0), nt(local, leaving), 0.0)
    shape = (flat, flat)
    stay = keep(step_of(shape, 0) == step_of(shape, 1), nt(local, slot_steps))
    for x in range(PARTS):
        piece_q = nn(stay, q_ref[:, x * piece:(x + 1) * piece])
        piece_q = piece_q + nn(keep(b_part == x, moved), got[:, :piece])
        for hh in range(piece // HD):
            h = x * (piece // HD) + hh
            for s in range(steps):
                row = (h // group) * steps * group + s * group + h % group
                q3[:, row, :] = piece_q[s * slots:(s + 1) * slots, hh * HD:(hh + 1) * HD]
    shape = (flat, 2 * flat)
    f_step, f_kv = fresh_of(shape, 1)
    stay = jnp.where(step_of(shape, 0) == f_step, nt(local, slot_kv), 0.0)
    for which in range(2):
        for g in range(heads):
            fresh = nn(keep(f_kv == which, stay), kv_ref[:, g * HD:(g + 1) * HD])
            fresh = fresh + nn(keep(b_part == which * heads + g, moved), got[:, piece:])
            kn[which, :, g * HD:(g + 1) * HD] = fresh.astype(BF16)

    inverse = 1.0 / math.sqrt(HD)
    head_rows = steps * group
    q_row = iota((per * rows, HD), 0) & (rows - 1)
    n_row = iota((rows, flat), 0) & (head_rows - 1)
    n_step = split(n_row, group, steps)
    n_col = iota((rows, flat), 1)
    n_new = split(n_col, slots, steps)
    n_request = n_col - slots * n_new
    seen = n_new <= n_step
    place_t = iota((rows, cap), 1)

    @pl.loop(0, chunks)
    def _(part):
        load_cache(1, part).wait()

        @pl.loop(0, chunk // per)
        def _(p):
            start = part * chunk + p * per
            dequantize(1, start)
            q = q3[pl.ds(start, per)].reshape(per * rows, HD)
            q = jnp.concatenate(
                [
                    jnp.where((q_row >= g * head_rows) & (q_row < (g + 1) * head_rows), q, 0.0)
                    for g in range(heads)
                ],
                axis=1,
            ).astype(BF16)
            fresh = nt(q, kn[0]) * inverse
            for i in range(per):
                request = start + i
                q_i = q[i * rows:(i + 1) * rows]
                scores = nt(q_i, cache[0, request]) * inverse
                scores = jnp.where(place_t < len_ref[first + request], scores, -1e30)
                new = fresh[i * rows:(i + 1) * rows]
                new = jnp.where(seen & (n_request == request), new, -1e30)
                top = jnp.maximum(
                    jnp.max(scores, axis=1, keepdims=True), jnp.max(new, axis=1, keepdims=True)
                )
                exp_cache = jnp.exp(scores - top)
                exp_new = jnp.exp(new - top)
                scale_by = 1.0 / (
                    jnp.sum(exp_cache, axis=1, keepdims=True)
                    + jnp.sum(exp_new, axis=1, keepdims=True)
                )
                context = nn((exp_cache * scale_by).astype(BF16), cache[1, request])
                context = context + nn((exp_new * scale_by).astype(BF16), kn[1])
                for g in range(heads):
                    c3[request, g * head_rows:(g + 1) * head_rows, :] = context[
                        g * head_rows:(g + 1) * head_rows, g * HD:(g + 1) * HD
                    ]

    shape = (flat, flat)
    stay = keep(step_of(shape, 0) == step_of(shape, 1), nt(slot_steps, local))
    shape = (n_bucket, flat)
    _, b_step, _, _ = bucket_fields(shape, 0)
    move = keep(b_step == step_of(shape, 1), nt(leaving, local))
    for h in range(q_width // HD):
        at = (h // group) * steps * group + h % group
        context = jnp.concatenate([c3[:, at + s * group, :] for s in range(steps)], axis=0)
        context = context.astype(BF16)
        lhs[:flat, h * HD:(h + 1) * HD] = nn(stay, context).astype(BF16)
        lhs[flat:, h * HD:(h + 1) * HD] = nn(move, context).astype(BF16)

    def main_copy(k_slot, other, slot):
        return pltpu.make_async_remote_copy(
            src_ref=msend.at[k_slot], dst_ref=mrecv.at[slot],
            send_sem=ms_sem.at[k_slot], recv_sem=mr_sem.at[slot],
            device_id={"inst": me_i, "tp": other}, device_id_type=MESH,
        )

    def bucket_copy(k_slot, inst, tp, from_inst, from_tp):
        return pltpu.make_async_remote_copy(
            src_ref=bsend.at[k_slot, inst], dst_ref=brecv.at[from_inst, from_tp],
            send_sem=bs_sem.at[k_slot, inst], recv_sem=br_sem.at[from_inst, from_tp],
            device_id={"inst": inst, "tp": tp}, device_id_type=MESH,
        )

    _, _, _, b_part = bucket_fields((n_bucket, quarter), 0)

    def project(k, keep_main):
        load_weight(k).wait()
        moved_rows = jnp.zeros((n_bucket, quarter), F32)
        for x in range(PARTS):
            cols = slice(x * quarter, (x + 1) * quarter)
            part = nn(lhs[...], wbuf[k, :, cols])
            keep_main(x, cols, part[:flat])
            moved_rows = jnp.where(b_part == x, part[flat:], moved_rows)
        bsend[k] = moved_rows.astype(BF16).reshape(n_inst, bucket, quarter)

    def send_buckets(k, tp):
        @pl.loop(1, n_inst)
        def _(offset):
            bucket_copy(k, lax.rem(me_i + offset, n_inst), tp, me_i, me_t).start()

    @pl.loop(0, n_tp - 1)
    def _(k):
        tp = lax.rem(me_t + 1 + k, n_tp)

        def keep_main(x, cols, values):
            msend[k, :, cols] = values.astype(BF16)

        project(k, keep_main)
        main_copy(k, tp, me_t).start()
        send_buckets(k, tp)

    def keep_own(x, cols, values):
        own[:, cols] = values

    project(n_tp - 1, keep_own)
    send_buckets(n_tp - 1, me_t)

    others = [lax.rem(me_t + 1 + k, n_tp) for k in range(n_tp - 1)]
    for k in range(n_tp - 1):
        copy = main_copy(k, others[k], others[k])
        copy.wait_send()
        copy.wait_recv()

    @pl.loop(1, n_inst)
    def _(offset):
        inst = lax.rem(me_i + offset, n_inst)

        @pl.loop(0, n_tp)
        def _(k):
            copy = bucket_copy(k, inst, me_t, inst, k)
            copy.wait_send()
            copy.wait_recv()

    came = jnp.zeros((n_inst, bucket, quarter), F32)
    for t in range(n_tp):
        came = came + brecv[:, t].astype(F32)
    came = came.astype(BF16).reshape(n_bucket, quarter)
    shape = (flat, n_bucket)
    _, b_step, _, b_part2 = bucket_fields(shape, 1)
    put = jnp.where(step_of(shape, 0) == b_step, nt(slot_steps, arriving), 0.0)
    for x in range(PARTS):
        cols = slice(x * quarter, (x + 1) * quarter)
        done = own[:, cols] + nn(keep(b_part2 == x, put), came)
        for tp in others:
            done = done + mrecv[tp, :, cols].astype(F32)
        at = pl.multiple_of(me_t * block + x * quarter, quarter)
        out_ref[:, pl.ds(at, quarter)] = done.astype(BF16)

    def final_copy(k, other, owner):
        span = pl.ds(pl.multiple_of(owner * block, block), block)
        return pltpu.make_async_remote_copy(
            src_ref=out_ref.at[:, span], dst_ref=out_ref.at[:, span],
            send_sem=as_sem.at[k], recv_sem=ar_sem.at[owner],
            device_id={"inst": me_i, "tp": other}, device_id_type=MESH,
        )

    for k in range(n_tp - 1):
        final_copy(k, lax.rem(me_t + 1 + k, n_tp), me_t).start()
    for k in range(n_tp - 1):
        other = lax.rem(me_t + 1 + k, n_tp)
        final_copy(k, other, me_t).wait_send()
        final_copy(k, other, other).wait_recv()


def on_device(
    cache_base, cache_scale, outlier_tiles, outlier_pos, lengths, new_slot, queries, new_kv,
    out_weight,
):
    n_inst = lax.axis_size("inst")
    n_tp = lax.axis_size("tp")
    _, slots, cap, width = cache_base.shape
    steps, _, q_width = queries.shape
    n_req = new_slot.shape[0]
    out_width = out_weight.shape[1]
    tiles = cap // TILE
    chunk, per = 8, 4
    flat = steps * slots
    bucket = steps * MOVE * PARTS
    n_bucket = n_inst * bucket
    rows = q_width // HD * steps
    block = out_width // n_tp
    quarter = block // PARTS
    piece = q_width // PARTS
    chunks = slots // chunk
    vmem = pl.BlockSpec(memory_space=pltpu.VMEM)
    smem = pl.BlockSpec(memory_space=pltpu.SMEM)
    hbm = pl.BlockSpec(memory_space=pl.ANY)
    dma = pltpu.SemaphoreType.DMA
    out = pl.pallas_call(
        functools.partial(body, (n_inst, n_tp, slots, steps, chunk, per)),
        out_shape=jax.ShapeDtypeStruct((flat, out_width), BF16),
        in_specs=[vmem, smem, smem, vmem, vmem, hbm, hbm, hbm, hbm],
        out_specs=vmem,
        scratch_shapes=[
            pltpu.VMEM((2, slots, cap, width), BF16),
            pltpu.VMEM((2, slots * tiles, width), BF16),
            pltpu.VMEM((2, slots, TILE, width), BF16),
            pltpu.VMEM((n_tp, q_width, block), BF16),
            pltpu.VMEM((n_inst, bucket, piece + HD), BF16),
            pltpu.VMEM((n_inst, bucket, piece + HD), BF16),
            pltpu.VMEM((slots, rows, HD), F32),
            pltpu.VMEM((2, flat, width), BF16),
            pltpu.VMEM((slots, rows, HD), F32),
            pltpu.VMEM((flat + n_bucket, q_width), BF16),
            pltpu.VMEM((n_tp, flat, block), BF16),
            pltpu.VMEM((n_tp, flat, block), BF16),
            pltpu.VMEM((flat, block), F32),
            pltpu.VMEM((n_tp, n_inst, bucket, quarter), BF16),
            pltpu.VMEM((n_inst, n_tp, bucket, quarter), BF16),
            dma((2 * chunks + 2,)),
            dma((n_tp,)),
            dma((n_inst,)),
            dma((n_inst,)),
            dma((n_tp,)),
            dma((n_tp,)),
            dma((n_tp, n_inst)),
            dma((n_inst, n_tp)),
            dma((n_tp,)),
            dma((n_tp,)),
        ],
        compiler_params=pltpu.CompilerParams(
            collective_id=0, has_side_effects=True, vmem_limit_bytes=48 * 1024 * 1024
        ),
    )(
        new_slot.reshape(1, n_req),
        outlier_pos,
        lengths,
        queries.reshape(flat, q_width),
        new_kv.reshape(2 * flat, width),
        cache_base,
        cache_scale.reshape(2, slots * tiles, width),
        outlier_tiles,
        out_weight,
    )
    return out.reshape(steps, slots, out_width)


def solution(mesh):
    placed = (
        P(None, ("rep", "inst"), None, "tp"),
        P(None, ("rep", "inst"), None, "tp"),
        P(None, ("rep", "inst"), None, "tp"),
        P(None, "rep"),
        P("rep"),
        P("rep"),
        P(None, ("rep", "inst"), "tp"),
        P(None, None, ("rep", "inst"), "tp"),
        P("tp", None),
    )
    return jax.shard_map(
        on_device,
        mesh=mesh,
        in_specs=placed,
        out_specs=P(None, ("rep", "inst"), None),
        check_vma=False,
    )
```

time: 171 us -> 47 us (0.27)
  the two profiles are of different devices: /device:TPU:0 before, /device:TPU:27 now
where the time goes in v1:
time: 47 us; the launch traced here: 46.7 us
  Pallas kernels  40.2 us (86%)
  local copies, waits for them, and re-layouts  6.52 us (14%)
    pallas_call x1, Pallas kernels, on_device(): pl.pallas_call(functools.partial(body, (n_inst, n_tp, slots, steps, chunk...  40.2 us
    unnamed x15, local copies, waits for them, and re-layouts  6.52 us

profile of v1, /device:TPU:27, one launch (start us, length us, event | category | flops | bytes accessed | tf_op | source)
XLA Modules:
  0.0 46.7 jit_solution(1813070403857809664)
XLA Ops:
  0.0 0.0 copy-start
  0.0 1.1 %copy-done = bf16[2,24,32,256]{3,2,1,0:T(8,128)(2,1)S(1)} copy-done((bf16[2,24,32,256]{3,2,1,0:T(8,128)(2,1)S(1)}, bf16[2,24,32,256]{3,2,1,0:T(8,128)(2,1)}, u32[]{:S(2)}) %copy-start) | copy-done | bytes 786456
  1.1 0.0 copy-start.1
  1.1 0.9 %copy-done.1 = bf16[2,24,2048]{2,1,0:T(8,128)(2,1)S(1)} copy-done((bf16[2,24,2048]{2,1,0:T(8,128)(2,1)S(1)}, bf16[2,24,2048]{2,1,0:T(8,128)(2,1)}, u32[]{:S(2)}) %copy-start.1) | copy-done | bytes 196632
  2.1 0.0 copy-start.2
  2.1 0.9 %copy-done.2 = bf16[2,24,8,256]{3,2,1,0:T(8,128)(2,1)S(1)} copy-done((bf16[2,24,8,256]{3,2,1,0:T(8,128)(2,1)S(1)}, bf16[2,24,8,256]{3,2,1,0:T(8,128)(2,1)}, u32[]{:S(2)}) %copy-start.2) | copy-done | bytes 196632
  3.0 0.0 copy-start.3
  3.0 0.8 %copy-done.3 = bf16[2,2,24,256]{3,2,1,0:T(8,128)(2,1)S(1)} copy-done((bf16[2,2,24,256]{3,2,1,0:T(8,128)(2,1)S(1)}, bf16[2,2,24,256]{3,2,1,0:T(8,128)(2,1)}, u32[]{:S(2)}) %copy-start.3) | copy-done | bytes 49176
  3.8 0.0 copy-start.4
  3.8 0.7 %copy-done.4 = s32[2,96]{1,0:T(2,128)S(1)} copy-done((s32[2,96]{1,0:T(2,128)S(1)}, s32[2,96]{1,0:T(2,128)}, u32[]{:S(2)}) %copy-start.4) | copy-done | bytes 792
  4.5 0.0 copy-start.5
  4.5 0.7 %copy-done.5 = s32[96]{0:T(128)S(1)} copy-done((s32[96]{0:T(128)S(1)}, s32[96]{0:T(128)}, u32[]{:S(2)}) %copy-start.5) | copy-done | bytes 408
  5.1 0.0 copy-start.6
  5.1 0.7 %copy-done.6 = s32[96]{0:T(128)S(1)} copy-done((s32[96]{0:T(128)S(1)}, s32[96]{0:T(128)}, u32[]{:S(2)}) %copy-start.6) | copy-done | bytes 408
  5.8 40.2 %shard_map.91 = bf16[48,4096]{1,0:T(8,128)(2,1)S(1)} custom-call(s32[1,96]{1,0:T(1,128)S(1)} %bitcast.9, s32[2,96]{1,0:T(2,128)S(1)} %copy-done.4, s32[96]{0:T(128)S(1)} %copy-done.6, bf16[48,2048]{1,0:T(8,128)(2,1)S(1)} %bitcast.6, bf16[96,256]{1,0:T(8,128)(2,1)S(1)} %bitcast.8, bf16[2,24,256,256]{3,2,1,0:T(8,128)(2,1)} %base_hbm.1, ...), custom_call_target="tpu_custom_call" | custom-call | tf_op jit(solution)/shard_map/pallas_call | solution.py:415
  46.0 0.7 %copy.11 = bf16[2,24,4096]{2,1,0:T(8,128)(2,1)} copy(bf16[2,24,4096]{2,1,0:T(8,128)(2,1)S(1)} %bitcast.5) | data formatting | bytes 786432
Async XLA Ops:
  0.0 1.1 %copy-start = (bf16[2,24,32,256]{3,2,1,0:T(8,128)(2,1)S(1)}, bf16[2,24,32,256]{3,2,1,0:T(8,128)(2,1)}, u32[]{:S(2)}) copy-start(bf16[2,24,32,256]{3,2,1,0:T(8,128)(2,1)} %outl_hbm.1) | copy-start | bytes 2359300
  1.1 0.9 %copy-start.1 = (bf16[2,24,2048]{2,1,0:T(8,128)(2,1)S(1)}, bf16[2,24,2048]{2,1,0:T(8,128)(2,1)}, u32[]{:S(2)}) copy-start(bf16[2,24,2048]{2,1,0:T(8,128)(2,1)} %param.15) | copy-start | bytes 589828
  2.1 0.9 %copy-start.2 = (bf16[2,24,8,256]{3,2,1,0:T(8,128)(2,1)S(1)}, bf16[2,24,8,256]{3,2,1,0:T(8,128)(2,1)}, u32[]{:S(2)}) copy-start(bf16[2,24,8,256]{3,2,1,0:T(8,128)(2,1)} %param.10) | copy-start | bytes 589828
  3.0 0.8 %copy-start.3 = (bf16[2,2,24,256]{3,2,1,0:T(8,128)(2,1)S(1)}, bf16[2,2,24,256]{3,2,1,0:T(8,128)(2,1)}, u32[]{:S(2)}) copy-start(bf16[2,2,24,256]{3,2,1,0:T(8,128)(2,1)} %param.16) | copy-start | bytes 147460
  3.8 0.7 %copy-start.4 = (s32[2,96]{1,0:T(2,128)S(1)}, s32[2,96]{1,0:T(2,128)}, u32[]{:S(2)}) copy-start(s32[2,96]{1,0:T(2,128)} %pos_ref.1) | copy-start | bytes 2308
  4.5 0.7 %copy-start.5 = (s32[96]{0:T(128)S(1)}, s32[96]{0:T(128)}, u32[]{:S(2)}) copy-start(s32[96]{0:T(128)} %param.14) | copy-start | bytes 1156
  5.1 0.7 %copy-start.6 = (s32[96]{0:T(128)S(1)}, s32[96]{0:T(128)}, u32[]{:S(2)}) copy-start(s32[96]{0:T(128)} %len_ref.1) | copy-start | bytes 1156

commit v2 on v1

--- a/solution.py
+++ b/solution.py
@@ -42,11 +42,11 @@
 
 def body(
     dims,
-    ns_ref, pos_ref, len_ref, q_ref, kv_ref, base_hbm, scale_hbm, outl_hbm, w_hbm,
+    ns_hbm, pos_hbm, len_hbm, q_hbm, kv_hbm, base_hbm, scale_hbm, outl_hbm, w_hbm,
     out_ref,
-    cache, scale, outl, wbuf, qsend, qrecv, q3, kn, c3, lhs,
+    ns_ref, pos_ref, len_ref, q_ref, kv_ref, cache, scale, outl, wbuf, qsend, qrecv, q3, kn, c3, lhs,
     msend, mrecv, own, bsend, brecv,
-    load_sem, w_sem, qs_sem, qr_sem, ms_sem, mr_sem, bs_sem, br_sem, as_sem, ar_sem,
+    small_sem, load_sem, w_sem, qs_sem, qr_sem, ms_sem, mr_sem, bs_sem, br_sem, as_sem, ar_sem,
 ):
     n_inst, n_tp, slots, steps, chunk, per = dims
     me_i = lax.axis_index("inst")
@@ -68,6 +68,15 @@
     chunks = slots // chunk
     first = me_i * slots
 
+    small = [
+        pltpu.make_async_copy(src, dst, small_sem.at[i])
+        for i, (src, dst) in enumerate(
+            [(ns_hbm, ns_ref), (q_hbm, q_ref), (kv_hbm, kv_ref), (pos_hbm, pos_ref),
+             (len_hbm, len_ref)]
+        )
+    ]
+    for copy in small:
+        copy.start()
     n_dev = n_inst * n_tp
     me = me_i * n_tp + me_t
     barrier = pltpu.get_barrier_semaphore()
@@ -104,6 +113,7 @@
     for k in range(n_tp):
         load_weight(k).start()
 
+    small[0].wait()
     ns = ns_ref[...]
     lane = iota((1, n_req), 1)
     home = split(lane, slots, n_inst)
@@ -145,6 +155,8 @@
     def keep(mask, values):
         return jnp.where(mask, values, 0.0).astype(BF16)
 
+    small[1].wait()
+    small[2].wait()
     shape = (n_bucket, flat)
     _, b_step, _, b_part = bucket_fields(shape, 0)
     pick = keep(b_step == step_of(shape, 1), nt(arriving, slot_steps))
@@ -178,6 +190,8 @@
     for offset in range(1, n_inst):
         query_copy(lax.rem(me_i + offset, n_inst), me_i).start()
 
+    small[3].wait()
+    small[4].wait()
     load_scale.wait()
     load_outl.wait()
 
@@ -409,15 +423,19 @@
     piece = q_width // PARTS
     chunks = slots // chunk
     vmem = pl.BlockSpec(memory_space=pltpu.VMEM)
-    smem = pl.BlockSpec(memory_space=pltpu.SMEM)
     hbm = pl.BlockSpec(memory_space=pl.ANY)
     dma = pltpu.SemaphoreType.DMA
     out = pl.pallas_call(
         functools.partial(body, (n_inst, n_tp, slots, steps, chunk, per)),
         out_shape=jax.ShapeDtypeStruct((flat, out_width), BF16),
-        in_specs=[vmem, smem, smem, vmem, vmem, hbm, hbm, hbm, hbm],
+        in_specs=[hbm] * 9,
         out_specs=vmem,
         scratch_shapes=[
+            pltpu.VMEM((1, n_req), jnp.int32),
+            pltpu.SMEM((2, n_req), jnp.int32),
+            pltpu.SMEM((n_req,), jnp.int32),
+            pltpu.VMEM((flat, q_width), BF16),
+            pltpu.VMEM((2 * flat, width), BF16),
             pltpu.VMEM((2, slots, cap, width), BF16),
             pltpu.VMEM((2, slots * tiles, width), BF16),
             pltpu.VMEM((2, slots, TILE, width), BF16),
@@ -433,6 +451,7 @@
             pltpu.VMEM((flat, block), F32),
             pltpu.VMEM((n_tp, n_inst, bucket, quarter), BF16),
             pltpu.VMEM((n_inst, n_tp, bucket, quarter), BF16),
+            dma((5,)),
             dma((2 * chunks + 2,)),
             dma((n_tp,)),
             dma((n_inst,)),
@@ -445,7 +464,7 @@
             dma((n_tp,)),
         ],
         compiler_params=pltpu.CompilerParams(
-            collective_id=0, has_side_effects=True, vmem_limit_bytes=48 * 1024 * 1024
+            collective_id=0, has_side_effects=True, vmem_limit_bytes=63 * 1024 * 1024
         ),
     )(
         new_slot.reshape(1, n_req),

time: 47 us -> 42.2 us (0.90)
  local copies, waits for them, and re-layouts: 6.52 us -> 1.77 us
    unnamed x15 -> x1, local copies, waits for them, and re-layouts: 6.52 us -> 1.77 us
where the time goes in v2:
time: 42.2 us; the launch traced here: 42.1 us
  Pallas kernels  40.3 us (95%)
  local copies, waits for them, and re-layouts  1.77 us (4%)
    pallas_call x1, Pallas kernels, on_device(): pl.pallas_call(functools.partial(body, (n_inst, n_tp, slots, steps, chunk...  40.3 us
    unnamed x1, local copies, waits for them, and re-layouts  1.77 us

profile of v2, /device:TPU:27, one launch (start us, length us, event | category | flops | bytes accessed | tf_op | source)
XLA Modules:
  0.0 42.1 jit_solution(16941282766423933141)
XLA Ops:
  0.0 40.3 %shard_map.91 = bf16[48,4096]{1,0:T(8,128)(2,1)} custom-call(s32[1,96]{1,0:T(1,128)} %bitcast.9, s32[2,96]{1,0:T(2,128)} %pos_hbm.1, s32[96]{0:T(128)} %len_hbm.1, bf16[48,2048]{1,0:T(8,128)(2,1)} %bitcast.6, bf16[96,256]{1,0:T(8,128)(2,1)} %bitcast.8, bf16[2,24,256,256]{3,2,1,0:T(8,128)(2,1)} %base_hbm.1, bf16[2,192,256]{2,1,0:T(8,128)(2,1)} %bitcast.7, ...), custom_call_target="tpu_custom_call" | custom-call | tf_op jit(solution)/shard_map/pallas_call | solution.py:428
  40.3 1.8 %copy.11 = bf16[2,24,4096]{2,1,0:T(8,128)(2,1)} copy(bf16[2,24,4096]{2,1,0:T(8,128)(2,1)} %bitcast.5) | data formatting | bytes 786432
